TPU v7x, 128 devices: a whole 4x4x4 slice. The times are simulated.
128 devices in a mesh: grp: 4 (over z), fsdp: 32 (over y, x, core).
Axes of the slice: x: 4, y: 4, z: 4, core: 2. Of those that a mesh axis runs over, the one named last changes fastest.
Arguments:
- gradient: float32 [128, 262144], P(None, ('grp', 'fsdp')), may hold values from -1.5 to 1.5
- slot_block: int32 [256], replicated, may hold values from -1 to 127, as said below
- left_statistics: float32 [256, 512, 512], P(('grp', 'fsdp')), may hold values from -6 to 6
- right_statistics: float32 [256, 512, 512], P(('grp', 'fsdp')), may hold values from -6 to 6
- root_left: bfloat16 [256, 512, 512], P(('grp', 'fsdp')), may hold values from -2 to 2
- root_right: bfloat16 [256, 512, 512], P(('grp', 'fsdp')), may hold values from -2 to 2
Outputs:
- direction: bfloat16 [128, 262144], P(None, ('grp', 'fsdp'))
- new_left: float32 [256, 512, 512], P(('grp', 'fsdp'))
- new_right: float32 [256, 512, 512], P(('grp', 'fsdp'))
Inputs may be any that keep to these rules, and one draw needn't show every extreme that they name: `slot_block`: every block index 0 to 127 stands in exactly one slot; -1 marks a free slot. Slots q * 2 to q * 2 + 1 are those of device q along grp+fsdp. Devices own 0 to 2 blocks, and some device owns 2.
All inputs are finite; a program needn't handle non-finite values.
Results may differ from a plain program's by a relative error of at most 0.006.
Values may be sent and summed in bfloat16 or wider, within the bound.
A program may use at most 64 MiB of HBM per device.

v0:
```python
import jax
import jax.numpy as jnp
from jax import lax
from jax.sharding import PartitionSpec as P

decay_rate = 0.95
epsilon = 1e-06


def body(gradient, slot_block, left_statistics, right_statistics, root_left, root_right):
    groups = lax.axis_size("grp")
    members = lax.axis_size("fsdp")
    device_list = groups * members
    slots = left_statistics.shape[0]
    block_order = left_statistics.shape[1]
    blocks = gradient.shape[0]
    piece_len = gradient.shape[1]
    owner_table = slot_block.reshape(device_list, slots).T
    occupied = owner_table >= 0
    safe_index = jnp.maximum(owner_table, 0)
    selected = jnp.where(occupied[:, :, None], gradient[safe_index], 0.0)
    arrived = lax.all_to_all(
        selected.astype(jnp.bfloat16), ("grp", "fsdp"), split_axis=1, concat_axis=1, tiled=True
    ).astype(selected.dtype)
    arrived_tiles = arrived.reshape(slots, block_order, block_order)
    gram_left = jnp.einsum(
        "sij,skj->sik", arrived_tiles, arrived_tiles, precision=lax.Precision.HIGHEST
    )
    gram_right = jnp.einsum(
        "sji,sjk->sik", arrived_tiles, arrived_tiles, precision=lax.Precision.HIGHEST
    )
    new_left = decay_rate * left_statistics + gram_left
    new_right = decay_rate * right_statistics + gram_right
    tiles_half = arrived_tiles.astype(jnp.bfloat16)
    left_half = jnp.einsum(
        "sij,sjk->sik", root_left, tiles_half, preferred_element_type=jnp.float32
    ).astype(jnp.bfloat16)
    shaped = jnp.einsum("sij,sjk->sik", left_half, root_right, preferred_element_type=jnp.float32)
    grad_norm = jnp.sqrt(jnp.sum(arrived_tiles * arrived_tiles, axis=(1, 2)))
    shaped_norm = jnp.sqrt(jnp.sum(shaped * shaped, axis=(1, 2)))
    moved = (shaped * (grad_norm / (shaped_norm + epsilon))[:, None, None]).astype(jnp.bfloat16)
    returned = lax.all_to_all(
        moved.reshape(slots, device_list, piece_len),
        ("grp", "fsdp"),
        split_axis=1,
        concat_axis=1,
        tiled=True,
    )
    target = jnp.where(slot_block >= 0, slot_block, blocks)
    inverse = (
        jnp.zeros((blocks,), jnp.int32)
        .at[target]
        .set(jnp.arange(device_list * slots, dtype=jnp.int32), mode="drop")
    )
    position = inverse % slots * device_list + inverse // slots
    direction = returned.reshape(slots * device_list, piece_len)[position]
    return (direction, new_left, new_right)


def solution(mesh):
    placed = (
        P(None, ("grp", "fsdp")),
        P(),
        P(("grp", "fsdp"), None, None),
        P(("grp", "fsdp"), None, None),
        P(("grp", "fsdp"), None, None),
        P(("grp", "fsdp"), None, None),
    )
    return jax.shard_map(
        body,
        mesh=mesh,
        in_specs=placed,
        out_specs=(
            P(None, ("grp", "fsdp")),
            P(("grp", "fsdp"), None, None),
            P(("grp", "fsdp"), None, None),
        ),
        check_vma=False,
    )
```

profile of v0, /device:TPU:1, one launch (start us, length us, event | category | flops | bytes accessed | tf_op | source)
XLA Modules:
  0.0 82.9 jit_solution(4197002484906157466)
XLA Ops:
  0.6 0.0 copy-start
  0.6 0.8 compare_select_fusion
  1.4 0.7 broadcast_compare_fusion
  2.1 0.1 max.10
  2.2 0.1 copy.21
  2.3 0.2 ge.11
  2.5 3.6 %gather_fusion = bf16[256,2048]{1,0:T(8,128)(2,1)S(1)} fusion(f32[128,2048]{1,0:T(8,128)} %param.6, s32[1024]{0:T(1024)S(1)} %pad_clamp_fusion.1), kind=kCustom, calls=%fused_computation | custom fusion | bytes 2098176 | tf_op jit(solution)/shard_map/gather | solution.py:21
  6.1 4.0 %fusion = bf16[2,128,2048]{2,0,1:T(2,128)(2,1)} fusion(bf16[2,128,2048]{2,1,0:T(8,128)(2,1)S(1)} %bitcast.13, pred[2,128]{0,1:T(8,128)(4,1)S(1)} %bitcast.15), kind=kLoop, calls=%fused_computation.4 | loop fusion | flops 524288 | bytes 2097408 | tf_op jit(solution)/shard_map/convert_element_type | solution.py:23
  10.1 11.5 %all-to-all-start = ((bf16[2,128,2048]{2,0,1:T(2,128)(2,1)}), bf16[2,128,2048]{2,0,1:T(2,128)(2,1)S(1)}, u32[]{:S(2)}, u32[]{:S(2)}) async-start(bf16[2,128,2048]{2,0,1:T(2,128)(2,1)} %fusion), calls=%async_computation | async-start | bytes 2097152 | tf_op jit(solution)/shard_map/all_to_all | solution.py:22
  21.6 1.4 %scatter_custom_fusion = s32[128]{0:T(128)S(1)} fusion(s32[256]{0:T(256)S(1)} %get-tuple-element.3, s32[256]{0:T(256)S(1)} %iota.3, s32[]{:T(128)} %constant.34.clone.1), kind=kCustom, calls=%fused_computation.26 | custom fusion | bytes 516 | tf_op jit(solution)/shard_map/scatter | solution.py:53
  23.0 17.9 %all-to-all-done = bf16[2,128,2048]{2,0,1:T(2,128)(2,1)S(1)} async-done(((bf16[2,128,2048]{2,0,1:T(2,128)(2,1)}), bf16[2,128,2048]{2,0,1:T(2,128)(2,1)S(1)}, u32[]{:S(2)}, u32[]{:S(2)}) %all-to-all-start) | async-done | bytes 1048608 | tf_op jit(solution)/shard_map/all_to_all | solution.py:22
  40.9 1.3 %copy.23 = bf16[2,128,2048]{2,1,0:T(8,128)(2,1)} copy(bf16[2,128,2048]{2,0,1:T(2,128)(2,1)S(1)} %all-to-all-done) | data formatting | bytes 2097152 | tf_op jit(solution)/shard_map/all_to_all | solution.py:22
  42.2 1.7 %convert_element_type.18 = bf16[2,512,512]{2,1,0:T(8,128)(2,1)S(1)} reshape(bf16[2,128,2048]{2,1,0:T(8,128)(2,1)} %copy.23) | data formatting | bytes 2097152 | tf_op jit(solution)/shard_map/convert_element_type | solution.py:34
  44.0 4.0 %multiply_reduce_fusion = (f32[2]{0:T(128)S(1)}, f32[2,512,512]{2,1,0:T(8,128)}) fusion(bf16[2,512,512]{2,1,0:T(8,128)(2,1)S(1)} %copy-done, bf16[2,512,512]{2,1,0:T(8,128)(2,1)S(1)} %convert_element_type.18, bf16[2,512,512]{2,1,0:T(8,128)(2,1)} %param.10), kind=kOutput, calls=%fused_computation.8 | convolution fusion | flops 1075314688 | bytes 5242888 | tf_op jit(solution)/shard_map/sij,sjk->sik/dot_general | solution.py:38
  48.0 2.3 %multiply_reduce_fusion.1 = f32[2]{0:T(128)S(1)} fusion(bf16[2,128,2048]{2,0,1:T(2,128)(2,1)S(1)} %all-to-all-done), kind=kLoop, calls=%fused_computation.9 | loop fusion | flops 1572862 | bytes 1048584 | tf_op jit(solution)/shard_map/reduce_sum | solution.py:39
  50.2 1.9 %multiply_convert_fusion = bf16[2,512,512]{2,1,0:T(8,128)(2,1)S(1)} fusion(f32[2,512,512]{2,1,0:T(8,128)} %get-tuple-element.6, f32[2]{0:T(128)S(1)} %add_divide_fusion), kind=kLoop, calls=%fused_computation.7 | loop fusion | flops 1048576 | bytes 3145736 | tf_op jit(solution)/shard_map/convert_element_type | solution.py:41
  52.2 1.5 %reshape.28 = bf16[2,128,2048]{2,1,0:T(8,128)(2,1)} reshape(bf16[2,512,512]{2,1,0:T(8,128)(2,1)S(1)} %multiply_convert_fusion) | data formatting | bytes 2097152 | tf_op jit(solution)/shard_map/reshape | solution.py:43
  53.6 3.3 %copy.26 = bf16[2,128,2048]{2,0,1:T(2,128)(2,1)} copy(bf16[2,128,2048]{2,1,0:T(8,128)(2,1)} %reshape.28) | data formatting | bytes 2097152 | tf_op jit(solution)/shard_map/reshape | solution.py:43
  56.9 4.5 %all-to-all-start.1 = ((bf16[2,128,2048]{2,0,1:T(2,128)(2,1)}), bf16[2,128,2048]{2,0,1:T(2,128)(2,1)S(1)}, u32[]{:S(2)}, u32[]{:S(2)}) async-start(bf16[2,128,2048]{2,0,1:T(2,128)(2,1)} %copy.26), calls=%async_computation.1 | async-start | bytes 2097152 | tf_op jit(solution)/shard_map/all_to_all | solution.py:42
  61.4 3.8 %multiply_add_fusion = f32[2,512,512]{2,1,0:T(8,128)} fusion(f32[2,512,512]{2,1,0:T(8,128)} %param.9, bf16[2,512,512]{2,1,0:T(8,128)(2,1)S(1)} %convert_element_type.18), kind=kOutput, calls=%fused_computation.5 | convolution fusion | flops 537919488 | bytes 5242880 | tf_op jit(solution)/shard_map/sji,sjk->sik/dot_general | solution.py:29
  65.3 2.1 %multiply_add_fusion.1 = f32[2,512,512]{2,1,0:T(8,128)} fusion(f32[2,512,512]{2,1,0:T(8,128)S(1)} %copy-done.1, bf16[2,512,512]{2,1,0:T(8,128)(2,1)S(1)} %convert_element_type.18), kind=kOutput, calls=%fused_computation.6 | convolution fusion | flops 537919488 | bytes 5242880 | tf_op jit(solution)/shard_map/sij,skj->sik/dot_general | solution.py:26
  67.3 13.5 %all-to-all-done.1 = bf16[2,128,2048]{2,0,1:T(2,128)(2,1)S(1)} async-done(((bf16[2,128,2048]{2,0,1:T(2,128)(2,1)}), bf16[2,128,2048]{2,0,1:T(2,128)(2,1)S(1)}, u32[]{:S(2)}, u32[]{:S(2)}) %all-to-all-start.1) | async-done | bytes 1048608 | tf_op jit(solution)/shard_map/all_to_all | solution.py:42
  80.9 0.3 copy.27
  81.2 1.7 %gather_fusion.1 = bf16[128,2048]{1,0:T(8,128)(2,1)} fusion(bf16[256,2048]{1,0:T(8,128)(2,1)S(1)} %bitcast.12, s32[1024]{0:T(1024)S(1)} %pad_clamp_fusion), kind=kCustom, calls=%fused_computation.1 | custom fusion | bytes 1049088 | tf_op jit(solution)/shard_map/gather | solution.py:56
  (8 shorter events, 0.1 us)
Async XLA Ops:
  0.6 43.3 %copy-start = (bf16[2,512,512]{2,1,0:T(8,128)(2,1)S(1)}, bf16[2,512,512]{2,1,0:T(8,128)(2,1)}, u32[]{:S(2)}) copy-start(bf16[2,512,512]{2,1,0:T(8,128)(2,1)} %param.11) | copy-start | bytes 3145732
  10.1 30.8 %all-to-all-start = ((bf16[2,128,2048]{2,0,1:T(2,128)(2,1)}), bf16[2,128,2048]{2,0,1:T(2,128)(2,1)S(1)}, u32[]{:S(2)}, u32[]{:S(2)}) async-start(bf16[2,128,2048]{2,0,1:T(2,128)(2,1)} %fusion), calls=%async_computation | async-start | bytes 2097152 | tf_op jit(solution)/shard_map/all_to_all | solution.py:22
  56.9 24.0 %all-to-all-start.1 = ((bf16[2,128,2048]{2,0,1:T(2,128)(2,1)}), bf16[2,128,2048]{2,0,1:T(2,128)(2,1)S(1)}, u32[]{:S(2)}, u32[]{:S(2)}) async-start(bf16[2,128,2048]{2,0,1:T(2,128)(2,1)} %copy.26), calls=%async_computation.1 | async-start | bytes 2097152 | tf_op jit(solution)/shard_map/all_to_all | solution.py:42
  61.4 3.8 %copy-start.1 = (f32[2,512,512]{2,1,0:T(8,128)S(1)}, f32[2,512,512]{2,1,0:T(8,128)}, u32[]{:S(2)}) copy-start(f32[2,512,512]{2,1,0:T(8,128)} %param.8) | copy-start | bytes 6291460
where the time goes:
time: 83.4 us; the launch traced here: 82.9 us
  waiting for transfers between devices  31.5 us (38%)
  starting transfers between devices  16 us (19%)
  local copies, waits for them, and re-layouts  15.2 us (18%)
  matrix products  9.89 us (12%)
  other arithmetic  9.66 us (12%)
    all_to_all x1, waiting for transfers between devices, body(): lax.all_to_all(selected.astype(jnp.bfloat16), ('grp', 'fsdp'), split_axis...  17.9 us
    all_to_all x1, waiting for transfers between devices, body(): lax.all_to_all(moved.reshape(slots, device_list, piece_len), ('grp', 'fsd...  13.5 us
    all_to_all x1, starting transfers between devices, body(): lax.all_to_all(selected.astype(jnp.bfloat16), ('grp', 'fsdp'), split_axis...  11.5 us
    reshape x2, local copies, waits for them, and re-layouts, body(): moved.reshape(slots, device_list, piece_len)  4.74 us
    all_to_all x1, starting transfers between devices, body(): lax.all_to_all(moved.reshape(slots, device_list, piece_len), ('grp', 'fsd...  4.47 us
    dot_general x1, matrix products, body(): jnp.einsum('sij,sjk->sik', left_half, root_right, preferred_element_type=...  3.99 us
    convert_element_type x1, other arithmetic, body(): selected.astype(jnp.bfloat16)  3.98 us
    dot_general x1, matrix products, body(): jnp.einsum('sji,sjk->sik', arrived_tiles, arrived_tiles, precision=lax.Pr...  3.83 us
  transfers between devices with their start and end apart: 2, of which 2 were waited for; matrix products, arithmetic and copies ran while one was open for 9% of the time, Pallas kernels for 0%

commit v1 on v0

v1 whole, which is shorter than its diff:
```python
import jax
import jax.numpy as jnp
from jax import lax
from jax.experimental import pallas as pl
from jax.experimental.pallas import tpu as pltpu
from jax.sharding import PartitionSpec as P

decay_rate = 0.95
epsilon = 1e-06

BLOCKS = 128
SLOTS = 2
ORDER = 512
ROWS, LANES = 16, 128
GROUPS, Y, X, CORES = 4, 4, 4, 2
DEVICES = GROUPS * Y * X * CORES
LOGICAL = pl.DeviceIdType.LOGICAL


def far_first():
    ring = (0, 1, 2, 1)

    def hops(offset):
        return ring[offset // 32] + ring[offset // 8 % 4] + ring[offset // 2 % 4] + 0.1 * (offset % 2)

    return sorted(range(1, DEVICES), key=lambda offset: (-hops(offset), offset))


def kernel(
    slot_block, gradient, left_stat, right_stat, root_left, root_right,
    direction, new_left, new_right,
    rows_in, chunks_wide, chunks, outgoing, arrived, wide, tiles, half, moved, returned, wide_out,
    left_in, right_in, roots_l, roots_r, place_v, place_s,
    load_sem, stat_sem, place_sem, send_sem, recv_sem,
):
    g = lax.axis_index("grp")
    f = lax.axis_index("fsdp")
    me = g * 32 + f
    y, x, c = f // 8, lax.rem(f // 2, 4), lax.rem(f, 2)
    zs = [lax.rem(g + i, 4) * 32 for i in range(4)]
    ys = [lax.rem(y + i, 4) * 8 for i in range(4)]
    xs = [lax.rem(x + i, 4) * 2 for i in range(4)]
    cs = [lax.rem(c + i, 2) for i in range(2)]
    zy = [[a + b for b in ys] for a in zs]
    xc = [[a + b for b in cs] for a in xs]
    offsets = far_first()

    def device(offset):
        return zy[offset // 32][offset // 8 % 4] + xc[offset // 2 % 4][offset % 2]

    load = pltpu.make_async_copy(gradient, rows_in, load_sem.at[0])
    load.start()
    barrier = pltpu.get_barrier_semaphore()
    for offset in offsets:
        pl.semaphore_signal(barrier, inc=1, device_id=device(offset), device_id_type=LOGICAL)
    load_l = pltpu.make_async_copy(root_left, roots_l, load_sem.at[1])
    load_r = pltpu.make_async_copy(root_right, roots_r, load_sem.at[2])
    load_sl = pltpu.make_async_copy(left_stat, left_in, stat_sem.at[0])
    load_sr = pltpu.make_async_copy(right_stat, right_in, stat_sem.at[1])
    load_l.start()
    load_r.start()
    load_sl.start()
    load_sr.start()

    chunks[BLOCKS] = jnp.zeros((ROWS, LANES), jnp.bfloat16)
    load.wait()
    for j in range(ROWS):
        chunks_wide[pl.ds(j, BLOCKS, stride=ROWS), :] = rows_in[:, j * LANES : (j + 1) * LANES]

    def narrow(i, carry):
        chunks[pl.ds(i * 8, 8)] = (
            chunks_wide[pl.ds(pl.multiple_of(i * 128, 128), 128), :].astype(jnp.bfloat16).reshape(8, ROWS, LANES)
        )
        return carry

    lax.fori_loop(0, BLOCKS // 8, narrow, 0)

    def stage(s):
        def one(d, carry):
            block = slot_block[d * SLOTS + s]
            outgoing[s, d] = chunks[jnp.where(block < 0, BLOCKS, block)]
            return carry

        lax.fori_loop(0, DEVICES, one, 0, unroll=8)

    def send(i, source, target, s):
        for offset in offsets:
            d = device(offset)
            pltpu.make_async_remote_copy(
                src_ref=source.at[s, d],
                dst_ref=target.at[s, me],
                send_sem=send_sem.at[i],
                recv_sem=recv_sem.at[i],
                device_id=d,
                device_id_type=LOGICAL,
            ).start()
        target[s, me] = source[s, me]

    def wait(sems, i, buffer, s):
        part = buffer.at[s, pl.ds(0, DEVICES - 1)]
        pltpu.make_async_copy(part, part, sems.at[i]).wait()

    stage(0)
    pl.semaphore_wait(barrier, DEVICES - 1)
    send(0, outgoing, arrived, 0)
    stage(1)
    send(1, outgoing, arrived, 1)

    lanes = lax.broadcasted_iota(jnp.int32, (8, BLOCKS), 1)

    def find(q, found):
        return jnp.where(lanes == slot_block[q], q, found)

    place_v[...] = lax.fori_loop(0, DEVICES * SLOTS, find, jnp.zeros((8, BLOCKS), jnp.int32), unroll=8)
    place = pltpu.make_async_copy(place_v, place_s, place_sem)
    place.start()
    load_l.wait()
    load_r.wait()

    def precondition(s):
        def widen(i, carry):
            wide[pl.ds(pl.multiple_of(i * 128, 128), 128), :] = (
                arrived[s, pl.ds(i * 8, 8)].astype(jnp.float32).reshape(128, LANES)
            )
            return carry

        lax.fori_loop(0, DEVICES // 8, widen, 0)
        squares = jnp.zeros((8, LANES), jnp.float32)
        for j in range(ORDER // LANES):
            part = wide[pl.ds(j, ORDER, stride=4), :]
            squares += jnp.sum((part * part).reshape(ORDER // 8, 8, LANES), axis=0)
            tiles[s, :, j * LANES : (j + 1) * LANES] = part.astype(jnp.bfloat16)
        half[...] = jnp.dot(roots_l[s], tiles[s], preferred_element_type=jnp.float32).astype(jnp.bfloat16)
        shaped_squares = jnp.zeros((8, LANES), jnp.float32)
        for n in range(2):
            shaped = jnp.dot(
                half[...], roots_r[s, :, n * 256 : (n + 1) * 256], preferred_element_type=jnp.float32
            )
            for m in range(2):
                part = shaped[:, m * LANES : (m + 1) * LANES]
                shaped_squares += jnp.sum((part * part).reshape(ORDER // 8, 8, LANES), axis=0)
                wide[pl.ds(n * 2 + m, ORDER, stride=4), :] = part
        grad_norm = jnp.sqrt(jnp.sum(squares, keepdims=True))
        shaped_norm = jnp.sqrt(jnp.sum(shaped_squares, keepdims=True))
        scale = grad_norm / (shaped_norm + epsilon)

        def pack(i, carry):
            moved[s, pl.ds(i * 8, 8)] = (
                (wide[pl.ds(pl.multiple_of(i * 128, 128), 128), :] * scale)
                .astype(jnp.bfloat16)
                .reshape(8, ROWS, LANES)
            )
            return carry

        lax.fori_loop(0, DEVICES // 8, pack, 0)

    for s in range(SLOTS):
        wait(recv_sem, s, arrived, s)
        precondition(s)
        send(2 + s, moved, returned, s)

    load_sl.wait()
    load_sr.wait()
    for s in range(SLOTS):
        tile = tiles[s]
        new_left[s] = decay_rate * left_in[s] + lax.dot_general(
            tile, tile, (((1,), (1,)), ((), ())), preferred_element_type=jnp.float32
        )
        new_right[s] = decay_rate * right_in[s] + lax.dot_general(
            tile, tile, (((0,), (0,)), ((), ())), preferred_element_type=jnp.float32
        )
    place.wait()
    wait(recv_sem, 2, returned, 0)
    wait(recv_sem, 3, returned, 1)

    def gather(k, carry):
        q = place_s[0, k]
        wide_out[pl.ds(pl.multiple_of(k * ROWS, ROWS), ROWS), :] = returned[lax.rem(q, 2), q // 2].astype(jnp.float32)
        return carry

    lax.fori_loop(0, BLOCKS, gather, 0, unroll=8)
    for j in range(ROWS):
        direction[:, j * LANES : (j + 1) * LANES] = wide_out[pl.ds(j, BLOCKS, stride=ROWS), :].astype(jnp.bfloat16)
    for s in range(SLOTS):
        wait(send_sem, s, outgoing, s)
        wait(send_sem, 2 + s, moved, s)


def body(gradient, slot_block, left_statistics, right_statistics, root_left, root_right):
    anywhere = pl.BlockSpec(memory_space=pltpu.HBM)
    chunk = (ROWS, LANES)
    square = (SLOTS, ORDER, ORDER)
    flops = 2 * 4 * SLOTS * ORDER**3
    direction, new_left, new_right = pl.pallas_call(
        kernel,
        out_shape=(
            pltpu.VMEM((BLOCKS, ROWS * LANES), jnp.bfloat16),
            pltpu.VMEM(square, jnp.float32),
            pltpu.VMEM(square, jnp.float32),
        ),
        in_specs=[pl.BlockSpec(memory_space=pltpu.SMEM)] + [anywhere] * 5,
        out_specs=tuple(pl.BlockSpec(memory_space=pltpu.VMEM) for _ in range(3)),
        scratch_shapes=[
            pltpu.VMEM((BLOCKS, ROWS * LANES), jnp.float32),
            pltpu.VMEM((BLOCKS * ROWS, LANES), jnp.float32),
            pltpu.VMEM((BLOCKS + 1,) + chunk, jnp.bfloat16),
            pltpu.VMEM((SLOTS, DEVICES) + chunk, jnp.bfloat16),
            pltpu.VMEM((SLOTS, DEVICES) + chunk, jnp.bfloat16),
            pltpu.VMEM((DEVICES * ROWS, LANES), jnp.float32),
            pltpu.VMEM(square, jnp.bfloat16),
            pltpu.VMEM((ORDER, ORDER), jnp.bfloat16),
            pltpu.VMEM((SLOTS, DEVICES) + chunk, jnp.bfloat16),
            pltpu.VMEM((SLOTS, DEVICES) + chunk, jnp.bfloat16),
            pltpu.VMEM((BLOCKS * ROWS, LANES), jnp.float32),
            pltpu.VMEM(square, jnp.float32),
            pltpu.VMEM(square, jnp.float32),
            pltpu.VMEM(square, jnp.bfloat16),
            pltpu.VMEM(square, jnp.bfloat16),
            pltpu.VMEM((8, BLOCKS), jnp.int32),
            pltpu.SMEM((8, BLOCKS), jnp.int32),
            pltpu.SemaphoreType.DMA((3,)),
            pltpu.SemaphoreType.DMA((2,)),
            pltpu.SemaphoreType.DMA,
            pltpu.SemaphoreType.DMA((4,)),
            pltpu.SemaphoreType.DMA((4,)),
        ],
        compiler_params=pltpu.CompilerParams(
            collective_id=0, has_side_effects=True, vmem_limit_bytes=56 * 2**20
        ),
        cost_estimate=pl.CostEstimate(flops=flops, bytes_accessed=12 * 2**20, transcendentals=0),
    )(slot_block, gradient, left_statistics, right_statistics, root_left, root_right)
    return (direction, new_left, new_right)


def solution(mesh):
    placed = (
        P(None, ("grp", "fsdp")),
        P(),
        P(("grp", "fsdp"), None, None),
        P(("grp", "fsdp"), None, None),
        P(("grp", "fsdp"), None, None),
        P(("grp", "fsdp"), None, None),
    )
    return jax.shard_map(
        body,
        mesh=mesh,
        in_specs=placed,
        out_specs=(
            P(None, ("grp", "fsdp")),
            P(("grp", "fsdp"), None, None),
            P(("grp", "fsdp"), None, None),
        ),
        check_vma=False,
    )
```

time: 83.4 us -> 42.3 us (0.51)
  Pallas kernels: 0 us -> 38.1 us
  waiting for transfers between devices: 31.5 us -> 0 us
  starting transfers between devices: 16 us -> 0 us
  local copies, waits for them, and re-layouts: 15.2 us -> 3.43 us
  matrix products: 9.89 us -> 0 us
  other arithmetic: 9.66 us -> 0 us
    pallas_call x0 -> x1, Pallas kernels: none -> 38.1 us  [body(): pl.pallas_call(kernel, out_shape=(pltpu.VMEM((BLOCKS, ROWS * LANES), jnp....]
    all_to_all x2 -> x0, waiting for transfers between devices: 31.5 us -> none  [the longest x1 17.9 us: body(): lax.all_to_all(selected.astype(jnp.bfloat16), ('grp', 'fsdp'), split_axis...]
    all_to_all x2 -> x0, starting transfers between devices: 16 us -> none  [the longest x1 11.5 us: body(): lax.all_to_all(selected.astype(jnp.bfloat16), ('grp', 'fsdp'), split_axis...]
    dot_general x3 -> x0, matrix products: 9.89 us -> none  [the longest x1 3.99 us: body(): jnp.einsum('sij,sjk->sik', left_half, root_right, preferred_element_type=...]
    convert_element_type x2 -> x0, other arithmetic: 5.89 us -> none  [the longest x1 3.98 us: body(): selected.astype(jnp.bfloat16)]
    gather x2 -> x0, local copies, waits for them, and re-layouts: 5.31 us -> none  [the longest x1 3.59 us: body(): selected = jnp.where(occupied[:, :, None], gradient[safe_index], 0.0)]
    reshape x2 -> x0, local copies, waits for them, and re-layouts: 4.74 us -> none  [body(): moved.reshape(slots, device_list, piece_len)]
    unnamed x4 -> x3, local copies, waits for them, and re-layouts: 0.02 us -> 3.43 us
  transfers between devices with their start and end apart: 2 -> 0, of which waited for: 2 -> 0; matrix products, arithmetic and copies ran while one was open for 9% -> 0% of each run, Pallas kernels for 0% -> 0%
where the time goes in v1:
time: 42.3 us; the launch traced here: 42.2 us
  Pallas kernels  38.1 us (90%)
  local copies, waits for them, and re-layouts  3.43 us (8%)
  between operations  0.64 us (2%)
    pallas_call x1, Pallas kernels, body(): pl.pallas_call(kernel, out_shape=(pltpu.VMEM((BLOCKS, ROWS * LANES), jnp....  38.1 us
    unnamed x3, local copies, waits for them, and re-layouts  3.43 us

profile of v1, /device:TPU:1, one launch (start us, length us, event | category | flops | bytes accessed | tf_op | source)
XLA Modules:
  0.0 42.2 jit_solution(936825933060032926)
XLA Ops:
  0.6 38.1 %shard_map.85 = (bf16[128,2048]{1,0:T(8,128)(2,1)S(1)}, f32[2,512,512]{2,1,0:T(8,128)S(1)}, f32[2,512,512]{2,1,0:T(8,128)S(1)}) custom-call(s32[256]{0:T(256)} %slot_block.1, f32[128,2048]{1,0:T(8,128)} %gradient.1, f32[2,512,512]{2,1,0:T(8,128)} %left_stat.1, f32[2,512,512]{2,1,0:T(8,128)} %right_stat.1, bf16[2,512,512]{2,1,0:T(8,128)(2,1)} %root_left.1, ...), custom_call_target="tpu_custom_call" | custom-call | flops 2147483648 | bytes 12582912 | tf_op jit(solution)/shard_map/pallas_call | solution.py:194
  38.7 0.8 %copy.12 = bf16[128,2048]{1,0:T(8,128)(2,1)} copy(bf16[128,2048]{1,0:T(8,128)(2,1)S(1)} %get-tuple-element.3) | data formatting | bytes 1048576
  39.5 1.3 %copy.13 = f32[2,512,512]{2,1,0:T(8,128)} copy(f32[2,512,512]{2,1,0:T(8,128)S(1)} %get-tuple-element.4) | data formatting | bytes 4194304
  40.9 1.3 %copy.14 = f32[2,512,512]{2,1,0:T(8,128)} copy(f32[2,512,512]{2,1,0:T(8,128)S(1)} %get-tuple-element.5) | data formatting | bytes 4194304

commit v2 on v1

--- a/solution.py
+++ b/solution.py
@@ -28,10 +28,10 @@
 
 def kernel(
     slot_block, gradient, left_stat, right_stat, root_left, root_right,
-    direction, new_left, new_right,
-    rows_in, chunks_wide, chunks, outgoing, arrived, wide, tiles, half, moved, returned, wide_out,
-    left_in, right_in, roots_l, roots_r, place_v, place_s,
-    load_sem, stat_sem, place_sem, send_sem, recv_sem,
+    returned, new_left, new_right,
+    rows_in, chunks_wide, chunks, outgoing, arrived, wide, tiles, half, moved,
+    left_in, right_in, roots_l, roots_r,
+    load_sem, stat_sem, send_sem, recv_sem,
 ):
     g = lax.axis_index("grp")
     f = lax.axis_index("fsdp")
@@ -101,19 +101,11 @@
         pltpu.make_async_copy(part, part, sems.at[i]).wait()
 
     stage(0)
+    stage(1)
     pl.semaphore_wait(barrier, DEVICES - 1)
     send(0, outgoing, arrived, 0)
-    stage(1)
     send(1, outgoing, arrived, 1)
 
-    lanes = lax.broadcasted_iota(jnp.int32, (8, BLOCKS), 1)
-
-    def find(q, found):
-        return jnp.where(lanes == slot_block[q], q, found)
-
-    place_v[...] = lax.fori_loop(0, DEVICES * SLOTS, find, jnp.zeros((8, BLOCKS), jnp.int32), unroll=8)
-    place = pltpu.make_async_copy(place_v, place_s, place_sem)
-    place.start()
     load_l.wait()
     load_r.wait()
 
@@ -169,21 +161,37 @@
         new_right[s] = decay_rate * right_in[s] + lax.dot_general(
             tile, tile, (((0,), (0,)), ((), ())), preferred_element_type=jnp.float32
         )
-    place.wait()
     wait(recv_sem, 2, returned, 0)
     wait(recv_sem, 3, returned, 1)
-
-    def gather(k, carry):
-        q = place_s[0, k]
-        wide_out[pl.ds(pl.multiple_of(k * ROWS, ROWS), ROWS), :] = returned[lax.rem(q, 2), q // 2].astype(jnp.float32)
-        return carry
-
-    lax.fori_loop(0, BLOCKS, gather, 0, unroll=8)
-    for j in range(ROWS):
-        direction[:, j * LANES : (j + 1) * LANES] = wide_out[pl.ds(j, BLOCKS, stride=ROWS), :].astype(jnp.bfloat16)
     for s in range(SLOTS):
         wait(send_sem, s, outgoing, s)
         wait(send_sem, 2 + s, moved, s)
+
+
+def finish(slot_block, returned, left, right, direction, new_left, new_right, wide_out, rows_out, out_sem):
+    copies = [
+        pltpu.make_async_copy(source.at[s], target.at[s], out_sem.at[2 * i + s])
+        for i, (source, target) in enumerate(((left, new_left), (right, new_right)))
+        for s in range(SLOTS)
+    ]
+    for copy in copies:
+        copy.start()
+
+    def place(d, carry):
+        for s in range(SLOTS):
+            block = slot_block[d * SLOTS + s]
+            wide_out[jnp.where(block < 0, BLOCKS, block)] = returned[s, d].astype(jnp.float32)
+        return carry
+
+    lax.fori_loop(0, DEVICES, place, 0, unroll=8)
+    rows = wide_out.reshape((BLOCKS + 1) * ROWS, LANES)
+    for j in range(ROWS):
+        rows_out[:, j * LANES : (j + 1) * LANES] = rows[pl.ds(j, BLOCKS, stride=ROWS), :].astype(jnp.bfloat16)
+    last = pltpu.make_async_copy(rows_out, direction, out_sem.at[4])
+    last.start()
+    for copy in copies:
+        copy.wait()
+    last.wait()
 
 
 def body(gradient, slot_block, left_statistics, right_statistics, root_left, root_right):
@@ -191,10 +199,10 @@
     chunk = (ROWS, LANES)
     square = (SLOTS, ORDER, ORDER)
     flops = 2 * 4 * SLOTS * ORDER**3
-    direction, new_left, new_right = pl.pallas_call(
+    returned, left, right = pl.pallas_call(
         kernel,
         out_shape=(
-            pltpu.VMEM((BLOCKS, ROWS * LANES), jnp.bfloat16),
+            pltpu.VMEM((SLOTS, DEVICES) + chunk, jnp.bfloat16),
             pltpu.VMEM(square, jnp.float32),
             pltpu.VMEM(square, jnp.float32),
         ),
@@ -210,17 +218,12 @@
             pltpu.VMEM(square, jnp.bfloat16),
             pltpu.VMEM((ORDER, ORDER), jnp.bfloat16),
             pltpu.VMEM((SLOTS, DEVICES) + chunk, jnp.bfloat16),
-            pltpu.VMEM((SLOTS, DEVICES) + chunk, jnp.bfloat16),
-            pltpu.VMEM((BLOCKS * ROWS, LANES), jnp.float32),
             pltpu.VMEM(square, jnp.float32),
             pltpu.VMEM(square, jnp.float32),
             pltpu.VMEM(square, jnp.bfloat16),
             pltpu.VMEM(square, jnp.bfloat16),
-            pltpu.VMEM((8, BLOCKS), jnp.int32),
-            pltpu.SMEM((8, BLOCKS), jnp.int32),
             pltpu.SemaphoreType.DMA((3,)),
             pltpu.SemaphoreType.DMA((2,)),
-            pltpu.SemaphoreType.DMA,
             pltpu.SemaphoreType.DMA((4,)),
             pltpu.SemaphoreType.DMA((4,)),
         ],
@@ -229,7 +232,23 @@
         ),
         cost_estimate=pl.CostEstimate(flops=flops, bytes_accessed=12 * 2**20, transcendentals=0),
     )(slot_block, gradient, left_statistics, right_statistics, root_left, root_right)
-    return (direction, new_left, new_right)
+    in_vmem = pl.BlockSpec(memory_space=pltpu.VMEM)
+    return pl.pallas_call(
+        finish,
+        out_shape=(
+            jax.ShapeDtypeStruct((BLOCKS, ROWS * LANES), jnp.bfloat16),
+            jax.ShapeDtypeStruct(square, jnp.float32),
+            jax.ShapeDtypeStruct(square, jnp.float32),
+        ),
+        in_specs=[pl.BlockSpec(memory_space=pltpu.SMEM)] + [in_vmem] * 3,
+        out_specs=(anywhere,) * 3,
+        scratch_shapes=[
+            pltpu.VMEM((BLOCKS + 1,) + chunk, jnp.float32),
+            pltpu.VMEM((BLOCKS, ROWS * LANES), jnp.bfloat16),
+            pltpu.SemaphoreType.DMA((5,)),
+        ],
+        compiler_params=pltpu.CompilerParams(vmem_limit_bytes=16 * 2**20),
+    )(slot_block, returned, left, right)
 
 
 def solution(mesh):

time: 42.3 us -> 39.8 us (0.941)
  local copies, waits for them, and re-layouts: 3.43 us -> 0.01 us
  Pallas kernels: 38.1 us -> 39 us
    unnamed x3 -> x2, local copies, waits for them, and re-layouts: 3.43 us -> 0.01 us
    pallas_call x1 -> x2, Pallas kernels: 38.1 us -> 39 us  [the longest x1 36.2 us: body(): pl.pallas_call(kernel, out_shape=(pltpu.VMEM((SLOTS, DEVICES) + chunk, jn...]
where the time goes in v2:
time: 39.8 us; the launch traced here: 39.6 us
  Pallas kernels  39 us (98%)
  between operations  0.66 us (2%)
    pallas_call x1, Pallas kernels, body(): pl.pallas_call(kernel, out_shape=(pltpu.VMEM((SLOTS, DEVICES) + chunk, jn...  36.2 us
    pallas_call x1, Pallas kernels, body(): pl.pallas_call(finish, out_shape=(jax.ShapeDtypeStruct((BLOCKS, ROWS * LA...  2.77 us

profile of v2, /device:TPU:1, one launch (start us, length us, event | category | flops | bytes accessed | tf_op | source)
XLA Modules:
  0.0 39.6 jit_solution(1674963655469443788)
XLA Ops:
  0.6 0.0 copy-start
  0.6 36.2 %shard_map.85 = (bf16[2,128,16,128]{3,2,1,0:T(8,128)(2,1)S(1)}, f32[2,512,512]{2,1,0:T(8,128)S(1)}, f32[2,512,512]{2,1,0:T(8,128)S(1)}) custom-call(s32[256]{0:T(256)} %slot_block.3, f32[128,2048]{1,0:T(8,128)} %gradient.1, f32[2,512,512]{2,1,0:T(8,128)} %left_stat.1, f32[2,512,512]{2,1,0:T(8,128)} %right_stat.1, bf16[2,512,512]{2,1,0:T(8,128)(2,1)} %root_left.1, ...), custom_call_target="tpu_custom_call" | custom-call | flops 2147483648 | bytes 12582912 | tf_op jit(solution)/shard_map/pallas_call | solution.py:202
  36.9 0.0 copy-done
  36.9 2.8 %shard_map.86 = (bf16[128,2048]{1,0:T(8,128)(2,1)}, f32[2,512,512]{2,1,0:T(8,128)}, f32[2,512,512]{2,1,0:T(8,128)}) custom-call(s32[256]{0:T(256)S(1)} %copy-done, bf16[2,128,16,128]{3,2,1,0:T(8,128)(2,1)S(1)} %get-tuple-element.6.returned, f32[2,512,512]{2,1,0:T(8,128)S(1)} %get-tuple-element.7.left, f32[2,512,512]{2,1,0:T(8,128)S(1)} %get-tuple-element.8.right), custom_call_target="tpu_custom_call" | custom-call | tf_op jit(solution)/shard_map/pallas_call | solution.py:236
Async XLA Ops:
  0.6 36.2 %copy-start = (s32[256]{0:T(256)S(1)}, s32[256]{0:T(256)}, u32[]{:S(2)}) copy-start(s32[256]{0:T(256)} %slot_block.3) | copy-start | bytes 3076

commit v3 on v2

--- a/solution.py
+++ b/solution.py
@@ -26,12 +26,16 @@
     return sorted(range(1, DEVICES), key=lambda offset: (-hops(offset), offset))
 
 
+def apart(offset):
+    return sum(step > 0 for step in (offset // 32, offset // 8 % 4, offset // 2 % 4))
+
+
 def kernel(
     slot_block, gradient, left_stat, right_stat, root_left, root_right,
     returned, new_left, new_right,
     rows_in, chunks_wide, chunks, outgoing, arrived, wide, tiles, half, moved,
     left_in, right_in, roots_l, roots_r,
-    load_sem, stat_sem, send_sem, recv_sem,
+    load_sem, stat_sem, send_sem, recv_sem, round_sem,
 ):
     g = lax.axis_index("grp")
     f = lax.axis_index("fsdp")
@@ -51,7 +55,9 @@
     load = pltpu.make_async_copy(gradient, rows_in, load_sem.at[0])
     load.start()
     barrier = pltpu.get_barrier_semaphore()
-    for offset in offsets:
+    near = [offset for offset in offsets if apart(offset) <= 2]
+    lines = [offset for offset in near if offset % 2 == 0 and apart(offset) == 1]
+    for offset in near:
         pl.semaphore_signal(barrier, inc=1, device_id=device(offset), device_id_type=LOGICAL)
     load_l = pltpu.make_async_copy(root_left, roots_l, load_sem.at[1])
     load_r = pltpu.make_async_copy(root_right, roots_r, load_sem.at[2])
@@ -83,7 +89,7 @@
 
         lax.fori_loop(0, DEVICES, one, 0, unroll=8)
 
-    def send(i, source, target, s):
+    def send(i, source, target, s, offsets=offsets):
         for offset in offsets:
             d = device(offset)
             pltpu.make_async_remote_copy(
@@ -94,7 +100,6 @@
                 device_id=d,
                 device_id_type=LOGICAL,
             ).start()
-        target[s, me] = source[s, me]
 
     def wait(sems, i, buffer, s):
         part = buffer.at[s, pl.ds(0, DEVICES - 1)]
@@ -102,8 +107,15 @@
 
     stage(0)
     stage(1)
-    pl.semaphore_wait(barrier, DEVICES - 1)
-    send(0, outgoing, arrived, 0)
+    for s in range(SLOTS):
+        arrived[s, me] = outgoing[s, me]
+    pl.semaphore_wait(barrier, len(near))
+    for offset in lines:
+        pl.semaphore_signal(round_sem, inc=1, device_id=device(offset), device_id_type=LOGICAL)
+    send(0, outgoing, arrived, 0, [offset for offset in offsets if apart(offset) == 2])
+    pl.semaphore_wait(round_sem, len(lines))
+    send(0, outgoing, arrived, 0, [offset for offset in offsets if apart(offset) == 3])
+    send(0, outgoing, arrived, 0, [offset for offset in offsets if apart(offset) <= 1])
     send(1, outgoing, arrived, 1)
 
     load_l.wait()
@@ -150,6 +162,7 @@
         wait(recv_sem, s, arrived, s)
         precondition(s)
         send(2 + s, moved, returned, s)
+        returned[s, me] = moved[s, me]
 
     load_sl.wait()
     load_sr.wait()
@@ -226,6 +239,7 @@
             pltpu.SemaphoreType.DMA((2,)),
             pltpu.SemaphoreType.DMA((4,)),
             pltpu.SemaphoreType.DMA((4,)),
+            pltpu.SemaphoreType.REGULAR,
         ],
         compiler_params=pltpu.CompilerParams(
             collective_id=0, has_side_effects=True, vmem_limit_bytes=56 * 2**20

time: 39.8 us -> 39.2 us (0.985)
  Pallas kernels: 39 us -> 38.4 us
    pallas_call x1, Pallas kernels: 36.2 us -> 35.6 us  [body(): pl.pallas_call(kernel, out_shape=(pltpu.VMEM((SLOTS, DEVICES) + chunk, jn...]
where the time goes in v3:
time: 39.2 us; the launch traced here: 39 us
  Pallas kernels  38.4 us (98%)
  between operations  0.66 us (2%)
    pallas_call x1, Pallas kernels, body(): pl.pallas_call(kernel, out_shape=(pltpu.VMEM((SLOTS, DEVICES) + chunk, jn...  35.6 us
    pallas_call x1, Pallas kernels, body(): pl.pallas_call(finish, out_shape=(jax.ShapeDtypeStruct((BLOCKS, ROWS * LA...  2.77 us

profile of v3, /device:TPU:1, one launch (start us, length us, event | category | flops | bytes accessed | tf_op | source)
XLA Modules:
  0.0 39.0 jit_solution(9019697982584222212)
XLA Ops:
  0.6 0.0 copy-start
  0.6 35.6 %shard_map.85 = (bf16[2,128,16,128]{3,2,1,0:T(8,128)(2,1)S(1)}, f32[2,512,512]{2,1,0:T(8,128)S(1)}, f32[2,512,512]{2,1,0:T(8,128)S(1)}) custom-call(s32[256]{0:T(256)} %slot_block.3, f32[128,2048]{1,0:T(8,128)} %gradient.1, f32[2,512,512]{2,1,0:T(8,128)} %left_stat.1, f32[2,512,512]{2,1,0:T(8,128)} %right_stat.1, bf16[2,512,512]{2,1,0:T(8,128)(2,1)} %root_left.1, ...), custom_call_target="tpu_custom_call" | custom-call | flops 2147483648 | bytes 12582912 | tf_op jit(solution)/shard_map/pallas_call | solution.py:215
  36.2 0.0 copy-done
  36.3 2.8 %shard_map.86 = (bf16[128,2048]{1,0:T(8,128)(2,1)}, f32[2,512,512]{2,1,0:T(8,128)}, f32[2,512,512]{2,1,0:T(8,128)}) custom-call(s32[256]{0:T(256)S(1)} %copy-done, bf16[2,128,16,128]{3,2,1,0:T(8,128)(2,1)S(1)} %get-tuple-element.6.returned, f32[2,512,512]{2,1,0:T(8,128)S(1)} %get-tuple-element.7.left, f32[2,512,512]{2,1,0:T(8,128)S(1)} %get-tuple-element.8.right), custom_call_target="tpu_custom_call" | custom-call | tf_op jit(solution)/shard_map/pallas_call | solution.py:250
Async XLA Ops:
  0.6 35.6 %copy-start = (s32[256]{0:T(256)S(1)}, s32[256]{0:T(256)}, u32[]{:S(2)}) copy-start(s32[256]{0:T(256)} %slot_block.3) | copy-start | bytes 3076

commit v4 on v3

--- a/solution.py
+++ b/solution.py
@@ -31,10 +31,10 @@
 
 
 def kernel(
-    slot_block, gradient, left_stat, right_stat, root_left, root_right,
+    blocks_in, gradient, left_stat, right_stat, root_left, root_right,
     returned, new_left, new_right,
     rows_in, chunks_wide, chunks, outgoing, arrived, wide, tiles, half, moved,
-    left_in, right_in, roots_l, roots_r,
+    left_in, right_in, roots_l, roots_r, slot_block,
     load_sem, stat_sem, send_sem, recv_sem, round_sem,
 ):
     g = lax.axis_index("grp")
@@ -54,6 +54,8 @@
 
     load = pltpu.make_async_copy(gradient, rows_in, load_sem.at[0])
     load.start()
+    fetch = pltpu.make_async_copy(blocks_in, slot_block, load_sem.at[3])
+    fetch.start()
     barrier = pltpu.get_barrier_semaphore()
     near = [offset for offset in offsets if apart(offset) <= 2]
     lines = [offset for offset in near if offset % 2 == 0 and apart(offset) == 1]
@@ -105,6 +107,7 @@
         part = buffer.at[s, pl.ds(0, DEVICES - 1)]
         pltpu.make_async_copy(part, part, sems.at[i]).wait()
 
+    fetch.wait()
     stage(0)
     stage(1)
     for s in range(SLOTS):
@@ -181,7 +184,7 @@
         wait(send_sem, 2 + s, moved, s)
 
 
-def finish(slot_block, returned, left, right, direction, new_left, new_right, wide_out, rows_out, out_sem):
+def finish(blocks_in, returned, left, right, direction, new_left, new_right, wide_out, rows_out, slot_block, out_sem):
     copies = [
         pltpu.make_async_copy(source.at[s], target.at[s], out_sem.at[2 * i + s])
         for i, (source, target) in enumerate(((left, new_left), (right, new_right)))
@@ -189,6 +192,10 @@
     ]
     for copy in copies:
         copy.start()
+
+    fetch = pltpu.make_async_copy(blocks_in, slot_block, out_sem.at[5])
+    fetch.start()
+    fetch.wait()
 
     def place(d, carry):
         for s in range(SLOTS):
@@ -219,7 +226,7 @@
             pltpu.VMEM(square, jnp.float32),
             pltpu.VMEM(square, jnp.float32),
         ),
-        in_specs=[pl.BlockSpec(memory_space=pltpu.SMEM)] + [anywhere] * 5,
+        in_specs=[anywhere] * 6,
         out_specs=tuple(pl.BlockSpec(memory_space=pltpu.VMEM) for _ in range(3)),
         scratch_shapes=[
             pltpu.VMEM((BLOCKS, ROWS * LANES), jnp.float32),
@@ -235,7 +242,8 @@
             pltpu.VMEM(square, jnp.float32),
             pltpu.VMEM(square, jnp.bfloat16),
             pltpu.VMEM(square, jnp.bfloat16),
-            pltpu.SemaphoreType.DMA((3,)),
+            pltpu.SMEM((DEVICES * SLOTS,), jnp.int32),
+            pltpu.SemaphoreType.DMA((4,)),
             pltpu.SemaphoreType.DMA((2,)),
             pltpu.SemaphoreType.DMA((4,)),
             pltpu.SemaphoreType.DMA((4,)),
@@ -254,12 +262,13 @@
             jax.ShapeDtypeStruct(square, jnp.float32),
             jax.ShapeDtypeStruct(square, jnp.float32),
         ),
-        in_specs=[pl.BlockSpec(memory_space=pltpu.SMEM)] + [in_vmem] * 3,
+        in_specs=[anywhere] + [in_vmem] * 3,
         out_specs=(anywhere,) * 3,
         scratch_shapes=[
             pltpu.VMEM((BLOCKS + 1,) + chunk, jnp.float32),
             pltpu.VMEM((BLOCKS, ROWS * LANES), jnp.bfloat16),
-            pltpu.SemaphoreType.DMA((5,)),
+            pltpu.SMEM((DEVICES * SLOTS,), jnp.int32),
+            pltpu.SemaphoreType.DMA((6,)),
         ],
         compiler_params=pltpu.CompilerParams(vmem_limit_bytes=16 * 2**20),
     )(slot_block, returned, left, right)

time: 39.2 us -> 37.8 us (0.964)
  Pallas kernels: 38.4 us -> 37.1 us
    pallas_call x1, Pallas kernels: 35.6 us -> 34.8 us  [body(): pl.pallas_call(kernel, out_shape=(pltpu.VMEM((SLOTS, DEVICES) + chunk, jn...]
    pallas_call x1, Pallas kernels: 2.77 us -> 2.29 us  [body(): pl.pallas_call(finish, out_shape=(jax.ShapeDtypeStruct((BLOCKS, ROWS * LA...]
where the time goes in v4:
time: 37.8 us; the launch traced here: 37.7 us
  Pallas kernels  37.1 us (98%)
  between operations  0.66 us (2%)
    pallas_call x1, Pallas kernels, body(): pl.pallas_call(kernel, out_shape=(pltpu.VMEM((SLOTS, DEVICES) + chunk, jn...  34.8 us
    pallas_call x1, Pallas kernels, body(): pl.pallas_call(finish, out_shape=(jax.ShapeDtypeStruct((BLOCKS, ROWS * LA...  2.29 us

profile of v4, /device:TPU:1, one launch (start us, length us, event | category | flops | bytes accessed | tf_op | source)
XLA Modules:
  0.0 37.7 jit_solution(17762540136779820571)
XLA Ops:
  0.6 0.0 copy-start
  0.6 34.8 %shard_map.85 = (bf16[2,128,16,128]{3,2,1,0:T(8,128)(2,1)S(1)}, f32[2,512,512]{2,1,0:T(8,128)S(1)}, f32[2,512,512]{2,1,0:T(8,128)S(1)}) custom-call(s32[256]{0:T(256)} %blocks_in.3, f32[128,2048]{1,0:T(8,128)} %gradient.1, f32[2,512,512]{2,1,0:T(8,128)} %left_stat.1, f32[2,512,512]{2,1,0:T(8,128)} %right_stat.1, bf16[2,512,512]{2,1,0:T(8,128)(2,1)} %root_left.1, ...), custom_call_target="tpu_custom_call" | custom-call | flops 2147483648 | bytes 12582912 | tf_op jit(solution)/shard_map/pallas_call | solution.py:222
  35.4 0.0 copy-done
  35.4 2.3 %shard_map.86 = (bf16[128,2048]{1,0:T(8,128)(2,1)}, f32[2,512,512]{2,1,0:T(8,128)}, f32[2,512,512]{2,1,0:T(8,128)}) custom-call(s32[256]{0:T(256)S(1)} %copy-done, bf16[2,128,16,128]{3,2,1,0:T(8,128)(2,1)S(1)} %get-tuple-element.6.returned, f32[2,512,512]{2,1,0:T(8,128)S(1)} %get-tuple-element.7.left, f32[2,512,512]{2,1,0:T(8,128)S(1)} %get-tuple-element.8.right), custom_call_target="tpu_custom_call" | custom-call | tf_op jit(solution)/shard_map/pallas_call | solution.py:258
Async XLA Ops:
  0.6 34.8 %copy-start = (s32[256]{0:T(256)S(1)}, s32[256]{0:T(256)}, u32[]{:S(2)}) copy-start(s32[256]{0:T(256)} %blocks_in.3) | copy-start | bytes 3076

commit v5 on v4

--- a/solution.py
+++ b/solution.py
@@ -58,7 +58,7 @@
     fetch.start()
     barrier = pltpu.get_barrier_semaphore()
     near = [offset for offset in offsets if apart(offset) <= 2]
-    lines = [offset for offset in near if offset % 2 == 0 and apart(offset) == 1]
+    lines = [2, 4, 6]
     for offset in near:
         pl.semaphore_signal(barrier, inc=1, device_id=device(offset), device_id_type=LOGICAL)
     load_l = pltpu.make_async_copy(root_left, roots_l, load_sem.at[1])
@@ -230,11 +230,11 @@
         out_specs=tuple(pl.BlockSpec(memory_space=pltpu.VMEM) for _ in range(3)),
         scratch_shapes=[
             pltpu.VMEM((BLOCKS, ROWS * LANES), jnp.float32),
-            pltpu.VMEM((BLOCKS * ROWS, LANES), jnp.float32),
+            pltpu.VMEM(((BLOCKS + 1) * ROWS, LANES), jnp.float32),
             pltpu.VMEM((BLOCKS + 1,) + chunk, jnp.bfloat16),
             pltpu.VMEM((SLOTS, DEVICES) + chunk, jnp.bfloat16),
             pltpu.VMEM((SLOTS, DEVICES) + chunk, jnp.bfloat16),
-            pltpu.VMEM((DEVICES * ROWS, LANES), jnp.float32),
+            pltpu.VMEM(((DEVICES + 1) * ROWS, LANES), jnp.float32),
             pltpu.VMEM(square, jnp.bfloat16),
             pltpu.VMEM((ORDER, ORDER), jnp.bfloat16),
             pltpu.VMEM((SLOTS, DEVICES) + chunk, jnp.bfloat16),

time: 37.8 us -> 37.7 us (level)
  no operation moved by 1% of the time
where the time goes in v5:
time: 37.7 us; the launch traced here: 37.6 us
  Pallas kernels  36.9 us (98%)
  between operations  0.66 us (2%)
    pallas_call x1, Pallas kernels, body(): pl.pallas_call(kernel, out_shape=(pltpu.VMEM((SLOTS, DEVICES) + chunk, jn...  34.7 us
    pallas_call x1, Pallas kernels, body(): pl.pallas_call(finish, out_shape=(jax.ShapeDtypeStruct((BLOCKS, ROWS * LA...  2.28 us

profile of v5, /device:TPU:1, one launch (start us, length us, event | category | flops | bytes accessed | tf_op | source)
XLA Modules:
  0.0 37.6 jit_solution(3154634805885063822)
XLA Ops:
  0.6 0.0 copy-start
  0.6 34.7 %shard_map.85 = (bf16[2,128,16,128]{3,2,1,0:T(8,128)(2,1)S(1)}, f32[2,512,512]{2,1,0:T(8,128)S(1)}, f32[2,512,512]{2,1,0:T(8,128)S(1)}) custom-call(s32[256]{0:T(256)} %blocks_in.3, f32[128,2048]{1,0:T(8,128)} %gradient.1, f32[2,512,512]{2,1,0:T(8,128)} %left_stat.1, f32[2,512,512]{2,1,0:T(8,128)} %right_stat.1, bf16[2,512,512]{2,1,0:T(8,128)(2,1)} %root_left.1, ...), custom_call_target="tpu_custom_call" | custom-call | flops 2147483648 | bytes 12582912 | tf_op jit(solution)/shard_map/pallas_call | solution.py:222
  35.3 0.0 copy-done
  35.3 2.3 %shard_map.86 = (bf16[128,2048]{1,0:T(8,128)(2,1)}, f32[2,512,512]{2,1,0:T(8,128)}, f32[2,512,512]{2,1,0:T(8,128)}) custom-call(s32[256]{0:T(256)S(1)} %copy-done, bf16[2,128,16,128]{3,2,1,0:T(8,128)(2,1)S(1)} %get-tuple-element.6.returned, f32[2,512,512]{2,1,0:T(8,128)S(1)} %get-tuple-element.7.left, f32[2,512,512]{2,1,0:T(8,128)S(1)} %get-tuple-element.8.right), custom_call_target="tpu_custom_call" | custom-call | tf_op jit(solution)/shard_map/pallas_call | solution.py:258
Async XLA Ops:
  0.6 34.7 %copy-start = (s32[256]{0:T(256)S(1)}, s32[256]{0:T(256)}, u32[]{:S(2)}) copy-start(s32[256]{0:T(256)} %blocks_in.3) | copy-start | bytes 3076

commit v6 on v5

--- a/solution.py
+++ b/solution.py
@@ -52,15 +52,15 @@
     def device(offset):
         return zy[offset // 32][offset // 8 % 4] + xc[offset // 2 % 4][offset % 2]
 
-    load = pltpu.make_async_copy(gradient, rows_in, load_sem.at[0])
-    load.start()
-    fetch = pltpu.make_async_copy(blocks_in, slot_block, load_sem.at[3])
-    fetch.start()
     barrier = pltpu.get_barrier_semaphore()
     near = [offset for offset in offsets if apart(offset) <= 2]
     lines = [2, 4, 6]
     for offset in near:
         pl.semaphore_signal(barrier, inc=1, device_id=device(offset), device_id_type=LOGICAL)
+    load = pltpu.make_async_copy(gradient, rows_in, load_sem.at[0])
+    load.start()
+    fetch = pltpu.make_async_copy(blocks_in, slot_block, load_sem.at[3])
+    fetch.start()
     load_l = pltpu.make_async_copy(root_left, roots_l, load_sem.at[1])
     load_r = pltpu.make_async_copy(root_right, roots_r, load_sem.at[2])
     load_sl = pltpu.make_async_copy(left_stat, left_in, stat_sem.at[0])

time: 37.7 us -> 37.7 us (level)
  no operation moved by 1% of the time
where the time goes in v6:
time: 37.7 us; the launch traced here: 37.6 us
  Pallas kernels  36.9 us (98%)
  between operations  0.66 us (2%)
    pallas_call x1, Pallas kernels, body(): pl.pallas_call(kernel, out_shape=(pltpu.VMEM((SLOTS, DEVICES) + chunk, jn...  34.6 us
    pallas_call x1, Pallas kernels, body(): pl.pallas_call(finish, out_shape=(jax.ShapeDtypeStruct((BLOCKS, ROWS * LA...  2.28 us

profile of v6, /device:TPU:1, one launch (start us, length us, event | category | flops | bytes accessed | tf_op | source)
XLA Modules:
  0.0 37.6 jit_solution(13582593550510101253)
XLA Ops:
  0.6 0.0 copy-start
  0.6 34.6 %shard_map.85 = (bf16[2,128,16,128]{3,2,1,0:T(8,128)(2,1)S(1)}, f32[2,512,512]{2,1,0:T(8,128)S(1)}, f32[2,512,512]{2,1,0:T(8,128)S(1)}) custom-call(s32[256]{0:T(256)} %blocks_in.3, f32[128,2048]{1,0:T(8,128)} %gradient.1, f32[2,512,512]{2,1,0:T(8,128)} %left_stat.1, f32[2,512,512]{2,1,0:T(8,128)} %right_stat.1, bf16[2,512,512]{2,1,0:T(8,128)(2,1)} %root_left.1, ...), custom_call_target="tpu_custom_call" | custom-call | flops 2147483648 | bytes 12582912 | tf_op jit(solution)/shard_map/pallas_call | solution.py:222
  35.3 0.0 copy-done
  35.3 2.3 %shard_map.86 = (bf16[128,2048]{1,0:T(8,128)(2,1)}, f32[2,512,512]{2,1,0:T(8,128)}, f32[2,512,512]{2,1,0:T(8,128)}) custom-call(s32[256]{0:T(256)S(1)} %copy-done, bf16[2,128,16,128]{3,2,1,0:T(8,128)(2,1)S(1)} %get-tuple-element.6.returned, f32[2,512,512]{2,1,0:T(8,128)S(1)} %get-tuple-element.7.left, f32[2,512,512]{2,1,0:T(8,128)S(1)} %get-tuple-element.8.right), custom_call_target="tpu_custom_call" | custom-call | tf_op jit(solution)/shard_map/pallas_call | solution.py:258
Async XLA Ops:
  0.6 34.6 %copy-start = (s32[256]{0:T(256)S(1)}, s32[256]{0:T(256)}, u32[]{:S(2)}) copy-start(s32[256]{0:T(256)} %blocks_in.3) | copy-start | bytes 3076
